TPU v7x, 32 devices: a whole 2x2x4 slice. The times are simulated.
32 devices in a mesh: blk: 4 (over y, x), tok: 8 (over z, core).
Axes of the slice: x: 2, y: 2, z: 4, core: 2. Of those that a mesh axis runs over, the one named last changes fastest.
Arguments:
- tokens: bfloat16 [8, 1024, 1664], P('tok', 'blk'), may hold values from -6 to 6
- segment_ids: int32 [8, 1024], P('tok'), may hold values from 0 to 7, as said below
- merge_index: int32 [8, 256, 4], P('tok'), may hold values from 0 to 1023, as said below
- segment_owner: int32 [8, 8], P('tok'), may hold values from 0 to 7, each once within a row
- ln1_gain: float32 [1664], replicated, may hold values from 0.1 to 1.9
- ln1_bias: float32 [1664], replicated, may hold values from -4 to 4
- w_qkv: bfloat16 [3, 1664, 1664], P(None, 'tok', 'blk'), may hold values from -0.15625 to 0.15625
- qkv_bias: float32 [3, 1664], P(None, 'blk'), may hold values from -6 to 6
- w_out: bfloat16 [1664, 1664], P('blk', 'tok'), may hold values from -0.15625 to 0.15625
- out_bias: float32 [1664], replicated, may hold values from -6 to 6
- ln2_gain: float32 [1664], replicated, may hold values from 0.1 to 1.9
- ln2_bias: float32 [1664], replicated, may hold values from -4 to 4
- w_fc1: bfloat16 [1664, 8192], P(None, 'blk'), may hold values from -0.15625 to 0.15625
- fc1_bias: float32 [8192], P('blk'), may hold values from -6 to 6
- w_fc2: bfloat16 [8192, 1664], P('blk'), may hold values from -0.0625 to 0.0625
- fc2_bias: float32 [1664], replicated, may hold values from -6 to 6
- ln3_gain: float32 [1664], replicated, may hold values from 0.1 to 1.9
- ln3_bias: float32 [1664], replicated, may hold values from -4 to 4
- w_proj: bfloat16 [6656, 1664], P('tok', 'blk'), may hold values from -0.078125 to 0.078125
- proj_bias: float32 [1664], P('blk'), may hold values from -6 to 6
Outputs:
- returned: bfloat16 [8, 8, 64, 1664], P('tok', None, None, 'blk')
Inputs may be any that keep to these rules, and one draw needn't show every extreme that they name: `segment_ids`: within a block each segment holds 4 to 256 tokens, one exactly 256; the four tokens of one row of merge_index share a segment. `merge_index`: the rows of one block name each token of the block exactly once. `segment_owner`: each block's row is a permutation of the owners.
All inputs are finite; a program needn't handle non-finite values.
Results may differ from a plain program's by a relative error of at most 0.015.
Values may be sent and summed in bfloat16 or wider, within the bound.
No kernel may reach another device: no remote copies, remote signals or barrier semaphores. Data moves between devices by JAX's collectives and lax.ppermute only.
A program may use at most 128 MiB of HBM per device.

v0:
```python
import math

import jax
import jax.numpy as jnp
from jax import lax
from jax.sharding import PartitionSpec as P

HD = 104


EPS = 1e-06


def layer_norm(input_tensors, scales, offset):
    input_tensors = input_tensors.astype(jnp.float32)
    center = input_tensors - jnp.mean(input_tensors, axis=-1, keepdims=True)
    spread = jnp.mean(center * center, axis=-1, keepdims=True)
    return center * lax.rsqrt(spread + EPS) * scales + offset


def body(
    tokens,
    segment_ids,
    merge_index,
    segment_owner,
    ln1_gain,
    ln1_bias,
    w_qkv,
    qkv_bias,
    w_out,
    out_bias,
    ln2_gain,
    ln2_bias,
    w_fc1,
    fc1_bias,
    w_fc2,
    fc2_bias,
    ln3_gain,
    ln3_bias,
    w_proj,
    proj_bias,
):
    tok_block = tokens[0]
    row_count = tok_block.shape[0]
    model_width = tok_block.shape[1]
    head_cols = w_qkv.shape[2]
    heads_here = head_cols // HD
    normed_one = layer_norm(tok_block, ln1_gain, ln1_bias).astype(jnp.bfloat16)
    normed_all = lax.all_gather(normed_one, "blk", axis=0, tiled=True)
    all_rows = normed_all.shape[0]
    columns = normed_all
    projected_qkv = jnp.einsum(
        "td,cde->cte",
        columns,
        lax.all_gather(w_qkv, "tok", axis=1, tiled=True),
        preferred_element_type=jnp.float32,
    )
    projected_qkv = (projected_qkv + qkv_bias[:, None, :]).astype(jnp.bfloat16)
    projected_qkv = projected_qkv.reshape(3, all_rows, heads_here, HD)
    key_rows = projected_qkv[1]
    values = projected_qkv[2]
    segment_row = segment_ids[0]
    q_block = min(512, all_rows)
    block_count = all_rows // q_block
    query_rows = projected_qkv[0].reshape(block_count, q_block, heads_here, HD)
    query_segs = segment_row.reshape(block_count, q_block)
    score_scale = 1.0 / math.sqrt(HD)

    def attend(input_tensors):
        query_part, query_seg = input_tensors
        scores = (
            jnp.einsum("qhe,khe->hqk", query_part, key_rows, preferred_element_type=jnp.float32)
            * score_scale
        )
        allowed = query_seg[:, None] == segment_row[None, :]
        weights = jnp.where(allowed[None], jnp.exp(scores), 0.0)
        attn_probs = (weights / jnp.sum(weights, axis=-1, keepdims=True)).astype(jnp.bfloat16)
        mixed = jnp.einsum("hqk,khe->qhe", attn_probs, values, preferred_element_type=jnp.float32)
        return mixed.astype(jnp.bfloat16)

    attended = lax.map(attend, (query_rows, query_segs)).reshape(all_rows, head_cols)
    out_full = lax.all_gather(w_out, "tok", axis=1, tiled=True)
    attn_rows = lax.psum_scatter(
        jnp.dot(attended, out_full, preferred_element_type=jnp.float32).astype(jnp.bfloat16),
        "blk",
        scatter_dimension=0,
        tiled=True,
    ).astype(jnp.float32)
    after_attn = tok_block.astype(jnp.float32) + attn_rows + out_bias
    normed_two = layer_norm(after_attn, ln2_gain, ln2_bias).astype(jnp.bfloat16)
    pre_act = (
        jnp.dot(
            lax.all_gather(normed_two, "blk", axis=0, tiled=True),
            w_fc1,
            preferred_element_type=jnp.float32,
        )
        + fc1_bias
    )
    hidden_act = jax.nn.gelu(pre_act, approximate=False).astype(jnp.bfloat16)
    partial_sum = jnp.dot(hidden_act, w_fc2, preferred_element_type=jnp.float32)
    own_start = lax.axis_index("blk") * row_count
    own_rows = lax.dynamic_slice_in_dim(partial_sum, own_start, row_count, 0) + after_attn
    partial_sum = lax.dynamic_update_slice_in_dim(partial_sum, own_rows, own_start, 0)
    summed = lax.psum(partial_sum.astype(jnp.bfloat16), "blk").astype(jnp.float32)
    layer_all = (summed + fc2_bias).astype(jnp.bfloat16)
    final_all = layer_norm(layer_all, ln3_gain, ln3_bias).astype(jnp.bfloat16)
    merge_rows = merge_index[0]
    merged_count = merge_rows.shape[0]
    merged = jnp.take(final_all, merge_rows.reshape(-1), axis=0).reshape(
        merged_count, 4 * model_width
    )
    columns = merged
    projected = jnp.dot(
        columns,
        lax.all_gather(w_proj, "tok", axis=0, tiled=True),
        preferred_element_type=jnp.float32,
    )
    projected = (projected + proj_bias).astype(jnp.bfloat16)
    tok_count = lax.axis_size("tok")
    slot_cap = 2 * merged_count // tok_count
    owners_here = segment_owner[0]
    seg_rows = jnp.take(segment_row, merge_rows[:, 0])
    seg_match = (
        seg_rows[:, None] == jnp.arange(owners_here.shape[0], dtype=jnp.int32)[None, :]
    ).astype(jnp.int32)
    owner_rows = jnp.sum(seg_match * owners_here[None, :], axis=1)
    segment_matches = (
        owner_rows[:, None] == jnp.arange(tok_count, dtype=jnp.int32)[None, :]
    ).astype(jnp.int32)
    before = jnp.cumsum(segment_matches, axis=0) - segment_matches
    order_in = jnp.sum(before * segment_matches, axis=1)
    target = owner_rows * slot_cap + order_in
    placed = (jnp.arange(tok_count * slot_cap, dtype=jnp.int32)[:, None] == target[None, :]).astype(
        jnp.bfloat16
    )
    outgoing = jnp.dot(placed, projected, preferred_element_type=jnp.float32).astype(jnp.bfloat16)
    outgoing = outgoing.reshape(tok_count, slot_cap, projected.shape[1])
    arrived = lax.all_to_all(outgoing, "tok", split_axis=0, concat_axis=0, tiled=True)
    return arrived[None]


def solution(mesh):
    placed = (
        P("tok", "blk", None),
        P("tok", None),
        P("tok", None, None),
        P("tok", None),
        P(),
        P(),
        P(None, "tok", "blk"),
        P(None, "blk"),
        P("blk", "tok"),
        P(),
        P(),
        P(),
        P(None, "blk"),
        P("blk"),
        P("blk", None),
        P(),
        P(),
        P(),
        P("tok", "blk"),
        P("blk"),
    )
    return jax.shard_map(
        body, mesh=mesh, in_specs=placed, out_specs=P("tok", None, None, "blk"), check_vma=False
    )
```

profile of v0, /device:TPU:0, one launch (start us, length us, event | category | flops | bytes accessed | tf_op | source)
XLA Modules:
  0.0 472.4 jit_solution(7413131425552293660)
XLA Ops:
  6.5 1.4 convert_reduce_fusion.1
  7.9 1.5 fusion.43
  9.5 2.5 fusion.46
  12.0 0.0 all-gather.9.cloned.1.call-start
  12.1 2.6 copy.33
  14.6 0.0 all-gather.11.cloned.1.call-start
  14.7 1.7 copy.37
  16.5 0.0 reduce-scatter.2.cloned.1.call-start
  16.5 0.6 broadcast.197
  17.1 0.7 reduce.6
  17.8 43.2 %all-gather.7.cloned.1.call-done = bf16[1024,1664]{1,0:T(8,128)(2,1)} async-done(((bf16[256,1664]{1,0:T(8,128)(2,1)}), bf16[1024,1664]{1,0:T(8,128)(2,1)}) %all-gather.7.cloned.1.call-update) | async-done | bytes 3407888 | tf_op jit(solution)/shard_map/all_gather | solution.py:49
  61.0 70.8 %all-gather.9.cloned.1.call-done = bf16[3,1664,416]{2,0,1:T(4,128)(2,1)} async-done(((bf16[3,208,416]{2,0,1:T(4,128)(2,1)}), bf16[3,1664,416]{2,0,1:T(4,128)(2,1)}) %all-gather.9.cloned.1.call-update) | async-done | bytes 4153360 | tf_op jit(solution)/shard_map/all_gather | solution.py:55
  131.8 9.2 %fusion.34 = bf16[3,1024,416]{1,2,0:T(8,128)(2,1)S(1)} fusion(f32[3,416]{1,0:T(4,128)S(1)} %copy-done.14, bf16[3,1664,416]{2,0,1:T(4,128)(2,1)} %all-gather.9.cloned.1.call-done, bf16[1024,1664]{1,0:T(8,128)(2,1)} %all-gather.7.cloned.1.call-done), kind=kOutput, calls=%fused_computation.53 | convolution fusion | flops 4255580160 | bytes 10122112 | tf_op jit(solution)/shard_map/td,cde->cte/dot_general | solution.py:52
  141.0 0.2 fusion.95
  141.2 0.6 reshape_squeeze.10
  141.8 0.1 copy.35
  141.9 12.9 %while.10 = (s32[]{:T(128)}, bf16[2,512,4,104]{1,3,2,0:T(8,128)(2,1)}, s32[2,512]{1,0:T(2,128)S(1)}, s32[1,1024]{1,0:T(1,128)S(1)}, bf16[2,512,4,104]{1,3,2,0:T(...) while((s32[]{:T(128)}, ...), condition=%wide.region_8.9_spmd, body=%wide.region_6.8_spmd.sunk | while | flops 887830528 | bytes 27748504 | solution.py:81
  142.4 0.4 broadcast_compare_fusion.2
  142.8 2.5 fusion.111
  145.3 2.4 fusion.112
  147.7 0.9 copy-done.5
  148.7 0.4 broadcast_compare_fusion.2
  149.0 2.5 fusion.111
  151.5 2.4 fusion.112
  154.0 0.9 copy-done.5
  154.9 2.0 copy.36
  156.9 0.2 copy.42
  157.1 0.9 all-gather.11.cloned.1.call-done
  158.0 5.5 %convolution_convert_fusion = bf16[1024,1664]{1,0:T(8,128)(2,1)} fusion(bf16[1024,416]{0,1:T(8,128)(2,1)S(1)} %bitcast.110, bf16[416,1664]{0,1:T(8,128)(2,1)} %all-gather.11.cloned.1.call-done), kind=kOutput, calls=%fused_computation.49 | convolution fusion | flops 1419378688 | bytes 5644288 | tf_op jit(solution)/shard_map/dot_general | solution.py:84
  163.4 0.0 all-gather.13.cloned.1.call-start
  163.5 45.8 %reduce-scatter.2.cloned.1.call-done = bf16[256,1664]{1,0:T(8,128)(2,1)} async-done(((bf16[1024,1664]{1,0:T(8,128)(2,1)}), bf16[256,1664]{1,0:T(8,128)(2,1)}) %reduce-scatter.2.cloned.1.call-update) | async-done | bytes 851984 | tf_op jit(solution)/shard_map/reduce_scatter | solution.py:83
  209.3 1.5 fusion.57
  210.8 1.6 multiply_reduce_fusion
  212.5 2.6 add_convert_fusion.2
  215.2 0.0 all-gather.15.cloned.1.call-start
  215.2 0.5 all-gather.15.cloned.1.call-update
  215.8 45.7 %all-gather.13.cloned.1.call-done = bf16[1024,1664]{1,0:T(8,128)(2,1)} async-done(((bf16[256,1664]{1,0:T(8,128)(2,1)}), bf16[1024,1664]{1,0:T(8,128)(2,1)}) %all-gather.13.cloned.1.call-update) | async-done | bytes 3407888 | tf_op jit(solution)/shard_map/all_gather | solution.py:93
  261.5 11.1 %fusion.96 = f32[1024,2048]{1,0:T(8,128)S(1)} fusion(bf16[1024,1664]{1,0:T(8,128)(2,1)} %all-gather.13.cloned.1.call-done, bf16[1664,2048]{1,0:T(8,128)(2,1)} %param.34), kind=kOutput, calls=%fused_computation.131 | convolution fusion | flops 6979321856 | bytes 18612224 | tf_op jit(solution)/shard_map/dot_general | solution.py:92
  272.6 28.8 %fusion.29 = f32[1024,1664]{1,0:T(8,128)S(1)} fusion(bf16[2048,1664]{1,0:T(8,128)(2,1)} %param.36, f32[1024,2048]{1,0:T(8,128)S(1)} %fusion.96, f32[2048]{0:T(1024)S(1)} %copy-done.15), kind=kOutput, calls=%fused_computation.48 | convolution fusion | flops 7117733888 | bytes 22028288 | tf_op jit(solution)/shard_map/dot_general | solution.py:100
  301.5 0.5 add_dynamic-update-slice_fusion
  302.0 2.1 convert_element_type.78
  304.1 0.1 copy.38
  304.2 0.1 reshape_squeeze.11
  304.3 1.4 gather_fusion
  305.7 0.1 select_reduce_fusion
  305.8 0.6 reduce-window.6
  306.4 0.2 slice_reduce_fusion
  306.7 0.2 copy.32
  306.9 0.9 broadcast_in_dim.40
  307.8 2.0 copy.41
  309.8 0.1 fusion.61
  309.9 15.1 %all-gather.15.cloned.1.call-done = bf16[8,832,416]{1,2,0:T(8,128)(2,1)} async-done(((bf16[1,832,416]{1,2,0:T(8,128)(2,1)}), bf16[8,832,416]{1,2,0:T(8,128)(2,1)}) %all-gather.15.cloned.1.call-update) | async-done | bytes 5537808 | tf_op jit(solution)/shard_map/all_gather | solution.py:115
  325.0 7.3 %copy.39 = bf16[8,832,416]{1,0,2:T(8,128)(2,1)} copy(bf16[8,832,416]{1,2,0:T(8,128)(2,1)} %all-gather.15.cloned.1.call-done) | data formatting | bytes 11075584 | tf_op jit(solution)/shard_map/all_gather | solution.py:115
  332.4 10.7 %reshape.179 = bf16[6656,416]{0,1:T(8,128)(2,1)} reshape(bf16[8,832,416]{1,0,2:T(8,128)(2,1)} %copy.39) | data formatting | bytes 11075584
  343.1 75.4 %all-reduce.2.cloned.1.call-done = bf16[1024,1664]{1,0:T(8,128)(2,1)} async-done(((bf16[1024,1664]{1,0:T(8,128)(2,1)}), bf16[1024,1664]{1,0:T(8,128)(2,1)}) %all-reduce.2.cloned.1.call-update) | async-done | bytes 3407888 | tf_op jit(solution)/shard_map/psum | solution.py:104
  418.5 2.9 convert_reduce_fusion
  421.3 3.2 fusion.23
  424.5 1.8 fusion.26
  426.4 5.9 %gather_fusion.1 = bf16[1024,1664]{1,0:T(8,128)(2,1)} fusion(bf16[1024,1664]{1,0:T(8,128)(2,1)S(1)} %fusion.26, s32[1024]{0:T(1024)S(1)} %broadcast_clamp_fusion), kind=kCustom, calls=%fused_computation.1 | custom fusion | bytes 6819840 | tf_op jit(solution)/shard_map/jit(_take)/gather | solution.py:109
  432.2 5.4 %gather.15 = bf16[256,6656]{1,0:T(8,128)(2,1)S(1)} reshape(bf16[1024,1664]{1,0:T(8,128)(2,1)} %gather_fusion.1) | data formatting | bytes 6815744 | tf_op jit(solution)/shard_map/jit(_take)/gather | solution.py:109
  437.7 5.9 %convolution_convert_fusion.1 = bf16[512,416]{0,1:T(8,128)(2,1)} fusion(bf16[6656,416]{0,1:T(8,128)(2,1)} %reshape.179, pred[256,6656]{1,0:T(8,128)(4,1)} %bitcast.107, bf16[256,6656]{1,0:T(8,128)(2,1)S(1)} %gather.15, s32[256]{0:T(256)S(1)} %multiply_add_fusion, f32[416]{0:T(512)S(1)} %copy-done.16), kind=kOutput, calls=%fused_computation.69 | convolution fusion | flops 1528987648 | bytes 11078272 | tf_op jit(solution)/shard_map/dot_general | solution.py:136
  443.5 1.2 copy.40
  444.8 19.8 %all_to_all.5 = bf16[8,64,416]{2,1,0:T(8,128)(2,1)S(1)} all-to-all(bf16[8,64,416]{2,1,0:T(8,128)(2,1)S(1)} %bitcast.105), channel_id=1, replica_groups=mesh['blk'=4,'tok'=8] {'tok'}, dimensions={0} | all-to-all | bytes 851968 | tf_op jit(solution)/shard_map/all_to_all | solution.py:138
  464.5 0.8 copy.57
  (64 shorter events, 0.4 us)
Async XLA Ops:
  6.5 10.6 %copy-start = (s32[1,1024]{1,0:T(1,128)S(1)}, s32[1,1024]{1,0:T(1,128)}, u32[]{:S(2)}) copy-start(s32[1,1024]{1,0:T(1,128)} %param.23) | copy-start | bytes 12292
  6.5 125.3 %copy-start.14 = (f32[3,416]{1,0:T(4,128)S(1)}, f32[3,416]{1,0:T(4,128)}, u32[]{:S(2)}) copy-start(f32[3,416]{1,0:T(4,128)} %param.29) | copy-start | bytes 14980
  6.5 54.5 %all-gather.7.cloned.1.call-start = ((), (), s32[]{:S(2)}) async-start(), calls=%async_computation.2 | async-start | bytes 4259840 | tf_op jit(solution)/shard_map/all_gather | solution.py:49
  12.0 119.8 %all-gather.9.cloned.1.call-start = ((), (), s32[]{:S(2)}) async-start(), calls=%async_computation.3 | async-start | bytes 7667712 | tf_op jit(solution)/shard_map/all_gather | solution.py:55
  14.6 143.3 %all-gather.11.cloned.1.call-start = ((), (), s32[]{:S(2)}) async-start(), calls=%async_computation.4 | async-start | bytes 1916928 | tf_op jit(solution)/shard_map/all_gather | solution.py:82
  16.5 192.8 %reduce-scatter.2.cloned.1.call-start = ((), (), s32[]{:S(2)}) async-start(), calls=%async_computation.5 | async-start | bytes 4259840 | tf_op jit(solution)/shard_map/reduce_scatter | solution.py:83
  142.4 2.9 copy-start.4
  147.7 0.9 copy-start.5
  148.7 2.9 copy-start.4
  153.9 0.9 copy-start.5
  158.0 51.3 %copy-start.1 = (bf16[1,256,1664]{2,1,0:T(8,128)(2,1)S(1)}, bf16[1,256,1664]{2,1,0:T(8,128)(2,1)}, u32[]{:S(2)}) copy-start(bf16[1,256,1664]{2,1,0:T(8,128)(2,1)} %param.22) | copy-start | bytes 2555908
  158.0 51.3 %copy-start.6 = (f32[1664]{0:T(1024)S(1)}, f32[1664]{0:T(1024)}, u32[]{:S(2)}) copy-start(f32[1664]{0:T(1024)} %param.31) | copy-start | bytes 19972
  163.4 49.1 %copy-start.9 = (f32[1664]{0:T(1024)S(1)}, f32[1664]{0:T(1024)}, u32[]{:S(2)}) copy-start(f32[1664]{0:T(1024)} %param.33) | copy-start | bytes 19972
  163.4 49.1 %copy-start.10 = (f32[1664]{0:T(1024)S(1)}, f32[1664]{0:T(1024)}, u32[]{:S(2)}) copy-start(f32[1664]{0:T(1024)} %param.32) | copy-start | bytes 19972
  163.4 98.0 %all-gather.13.cloned.1.call-start = ((), (), s32[]{:S(2)}) async-start(), calls=%async_computation.6 | async-start | bytes 4259840 | tf_op jit(solution)/shard_map/all_gather | solution.py:93
  215.2 109.9 %all-gather.15.cloned.1.call-start = ((), (), s32[]{:S(2)}) async-start(), calls=%async_computation.8 | async-start | bytes 6709248 | tf_op jit(solution)/shard_map/all_gather | solution.py:115
  215.7 202.7 %all-reduce.2.cloned.1.call-start = ((), (), s32[]{:S(2)}) async-start(), calls=%async_computation.7 | async-start | bytes 6815744 | tf_op jit(solution)/shard_map/psum | solution.py:104
  215.8 56.8 %copy-start.15 = (f32[2048]{0:T(1024)S(1)}, f32[2048]{0:T(1024)}, u32[]{:S(2)}) copy-start(f32[2048]{0:T(1024)} %param.35) | copy-start | bytes 24580
  272.6 28.9 %copy-start.3 = (bf16[256,1664]{1,0:T(8,128)(2,1)S(1)}, bf16[256,1664]{1,0:T(8,128)(2,1)}, u32[]{:S(2)}) copy-start(bf16[256,1664]{1,0:T(8,128)(2,1)} %reduce-scatter.2.cloned.1.call-done) | copy-start | bytes 2555908
  301.9 2.1 copy-start.8
  301.9 3.8 copy-start.13
  332.3 86.1 %copy-start.7 = (f32[1664]{0:T(1024)S(1)}, f32[1664]{0:T(1024)}, u32[]{:S(2)}) copy-start(f32[1664]{0:T(1024)} %param.37) | copy-start | bytes 19972
  332.3 92.2 %copy-start.11 = (f32[1664]{0:T(1024)S(1)}, f32[1664]{0:T(1024)}, u32[]{:S(2)}) copy-start(f32[1664]{0:T(1024)} %param.39) | copy-start | bytes 19972
  332.4 92.2 %copy-start.12 = (f32[1664]{0:T(1024)S(1)}, f32[1664]{0:T(1024)}, u32[]{:S(2)}) copy-start(f32[1664]{0:T(1024)} %param.38) | copy-start | bytes 19972
  418.4 6.1 %copy-start.2 = (bf16[1024,1664]{1,0:T(8,128)(2,1)S(1)}, bf16[1024,1664]{1,0:T(8,128)(2,1)}, u32[]{:S(2)}) copy-start(bf16[1024,1664]{1,0:T(8,128)(2,1)} %all-reduce.2.cloned.1.call-done) | copy-start | bytes 10223620
  432.2 5.4 %copy-start.16 = (f32[416]{0:T(512)S(1)}, f32[416]{0:T(512)}, u32[]{:S(2)}) copy-start(f32[416]{0:T(512)} %param.41) | copy-start | bytes 4996
Sparse Core Ops, SparseCore 0:
  12.1 48.8 all-gather.6
  62.7 69.0 all-gather.8
  133.4 24.4 all-gather.10
  163.6 45.6 reduce-scatter.1
  215.3 46.1 all-gather.12
  262.9 62.0 all-gather.14
  328.2 90.2 all-reduce.1
where the time goes:
time: 479 us; the launch traced here: 472 us
  waiting for transfers between devices  297 us (62%)
  matrix products  70.2 us (15%)
  local copies, waits for them, and re-layouts  46.2 us (10%)
  other arithmetic  24 us (5%)
  blocking collectives  19.8 us (4%)
  between operations  14 us (3%)
    psum x1, waiting for transfers between devices, body(): lax.psum(partial_sum.astype(jnp.bfloat16), 'blk').astype(jnp.float32)  75.4 us
    all_gather x1, waiting for transfers between devices, body(): lax.all_gather(w_qkv, 'tok', axis=1, tiled=True)  70.8 us
    reduce_scatter x1, waiting for transfers between devices, body(): lax.psum_scatter(jnp.dot(attended, out_full, preferred_element_type=jnp.f...  45.8 us
    all_gather x1, waiting for transfers between devices, body(): lax.all_gather(normed_two, 'blk', axis=0, tiled=True)  45.7 us
    all_gather x1, waiting for transfers between devices, body(): normed_all = lax.all_gather(normed_one, 'blk', axis=0, tiled=True)  43.2 us
    dot_general x1, matrix products, body(): partial_sum = jnp.dot(hidden_act, w_fc2, preferred_element_type=jnp.float32)  28.8 us
    all_to_all x1, blocking collectives, body(): lax.all_to_all(outgoing, 'tok', split_axis=0, concat_axis=0, tiled=True)  19.8 us
    unnamed x38, local copies, waits for them, and re-layouts  18.8 us
  transfers between devices with their start and end apart: 7, of which 7 were waited for; matrix products, arithmetic and copies ran while one was open for 20% of the time, Pallas kernels for 0%

commit v1 on v0

v1 whole, which is shorter than its diff:
```python
import functools
import math

import jax
import jax.numpy as jnp
from jax import lax
from jax.experimental import pallas as pl
from jax.experimental.pallas import tpu as pltpu
from jax.sharding import PartitionSpec as P

HD = 104
EPS = 1e-06
BF16 = jnp.bfloat16
F32 = jnp.float32
VMEM_LIMIT = 58 * 1024 * 1024
VM = pl.BlockSpec(memory_space=pltpu.VMEM)
SM = pl.BlockSpec(memory_space=pltpu.SMEM)
ANY = pl.BlockSpec(memory_space=pl.ANY)


def cost(flops, nbytes, trans=0):
    return pl.CostEstimate(flops=int(flops), bytes_accessed=int(nbytes), transcendentals=int(trans))


def params():
    return pltpu.CompilerParams(vmem_limit_bytes=VMEM_LIMIT)


def norm(x, gain, bias):
    center = x - jnp.mean(x, axis=-1, keepdims=True)
    spread = jnp.mean(center * center, axis=-1, keepdims=True)
    return center * lax.rsqrt(spread + EPS) * gain + bias


def swap(x, axis, mask):
    return lax.ppermute(x, axis, [(i, i ^ mask) for i in range(lax.axis_size(axis))])


def unxor(parts, index):
    bit = 1
    while bit < len(parts):
        hit = (index & bit) != 0
        parts = [jnp.where(hit, parts[i ^ bit], parts[i]) for i in range(len(parts))]
        bit *= 2
    return parts


def gather_blk(x):
    half = x.shape[0] // 2
    a, b = x[:half], x[half:]
    xa, yb = swap(a, "blk", 1), swap(b, "blk", 2)
    xb, ya = swap(b, "blk", 1), swap(a, "blk", 2)
    da, db = swap(xa, "blk", 2), swap(yb, "blk", 1)
    return jnp.concatenate([x, xa, xb, ya, yb, da, db], axis=0)


def same_core_groups(count):
    return [list(range(core, count, 2)) for core in range(2)]


def permute_norm_kernel(perm, place, tok, gain, bias, moved, normed):
    pick = (perm[...] == place[...]).astype(F32).astype(BF16)
    rows = jnp.dot(pick, tok[...], preferred_element_type=F32)
    moved[...] = rows.astype(BF16)
    normed[...] = norm(rows, gain[...], bias[...]).astype(BF16)


def permute_norm(perm, place, tok, gain, bias):
    rows, width = tok.shape
    step = 256
    return pl.pallas_call(
        permute_norm_kernel,
        grid=(rows // step,),
        in_specs=[
            pl.BlockSpec((step, 1), lambda i: (i, 0)),
            pl.BlockSpec((1, rows), lambda i: (0, 0)),
            pl.BlockSpec((rows, width), lambda i: (0, 0)),
            pl.BlockSpec((1, width), lambda i: (0, 0)),
            pl.BlockSpec((1, width), lambda i: (0, 0)),
        ],
        out_specs=[pl.BlockSpec((step, width), lambda i: (i, 0))] * 2,
        out_shape=[jax.ShapeDtypeStruct((rows, width), BF16)] * 2,
        compiler_params=params(),
        cost_estimate=cost(2 * rows * rows * width, 6 * rows * width),
        name="permute_norm",
    )(perm, place, tok, gain, bias)


def qkv_kernel(core, h, own, other, bias, out, weight, sems):
    groups, _, shard, _ = own.shape
    me = core[0]
    copies = []
    for z in range(groups):
        for n, (src, c) in enumerate(((own, me), (other, 1 - me))):
            start = pl.multiple_of((2 * z + c) * shard, 16)
            copy = pltpu.make_async_copy(src.at[z], weight.at[:, pl.ds(start, shard), :], sems.at[n, z])
            copy.start()
            copies.append(copy)
    for copy in copies:
        copy.wait()
    rows = h.shape[0]
    step = 256

    for part in range(3):

        @pl.loop(0, rows // step)
        def _(i):
            at = pl.ds(pl.multiple_of(i * step, step), step)
            acc = jnp.dot(h[at, :], weight[part], preferred_element_type=F32)
            out[part, at, :] = (acc + bias[part : part + 1, :]).astype(BF16)


def qkv_project(core, h, own, other, bias):
    groups, parts, shard, cols = own.shape
    rows, width = h.shape
    return pl.pallas_call(
        qkv_kernel,
        in_specs=[SM, VM, ANY, ANY, VM],
        out_specs=VM,
        out_shape=jax.ShapeDtypeStruct((parts, rows, cols), BF16),
        scratch_shapes=[
            pltpu.VMEM((parts, width, cols), BF16),
            pltpu.SemaphoreType.DMA((2, groups)),
        ],
        compiler_params=params(),
        cost_estimate=cost(2 * rows * width * parts * cols, 12e6),
        name="qkv_project",
    )(core, h, own, other, bias)


def attend_kernel(first, step, qkv, row_owner, col_owner, out):
    rows, cols = out.shape
    scale = math.log2(math.e) / math.sqrt(HD)
    keys = qkv.shape[1]
    for head in range(cols // HD):
        at = slice(head * HD, head * HD + HD)
        key = qkv[1, :, at]
        value = jnp.concatenate([qkv[2, :, at], jnp.ones((keys, 128 - HD), BF16)], axis=1)

        @pl.loop(0, rows // step)
        def _(i):
            mine = pl.ds(pl.multiple_of(i * step, step), step)
            query = qkv[0, pl.ds(pl.multiple_of(first + i * step, step), step), at]
            scores = lax.dot_general(query, key, (((1,), (1,)), ((), ())), preferred_element_type=F32)
            kept = row_owner[mine, :] == col_owner[...]
            weights = jnp.where(kept, jnp.exp2(scores * scale), 0.0).astype(BF16)
            mixed = jnp.dot(weights, value, preferred_element_type=F32)
            out[mine, at] = (mixed[:, :HD] / mixed[:, HD : HD + 1]).astype(BF16)


def attend(first, rows, qkv, row_owner, col_owner):
    _, keys, cols = qkv.shape
    return pl.pallas_call(
        functools.partial(attend_kernel, first, 256),
        in_specs=[VM] * 3,
        out_specs=VM,
        out_shape=jax.ShapeDtypeStruct((rows, cols), BF16),
        compiler_params=params(),
        cost_estimate=cost(4 * rows * keys * cols, 4e6, rows * keys * (cols // HD)),
        name="attend",
    )(qkv, row_owner, col_owner)


def mlp_kernel(
    where, att0, att1, att2, att3, tok, wo_own, wo_other, out_bias, gain, bias, w1, b1, w2, b2,
    mine, to1, to2, to3,
    wo, w1v, w2v, after, acc, sems_o, sems_1, sems_2,
):
    core, me = where[0], where[1]
    groups, shard, width = wo_own.shape
    tiles = sems_1.shape[0]
    tile = w1.shape[1] // tiles
    quarter = mine.shape[1]
    loads_o, loads_1, loads_2 = [], [], []
    for r in range(groups):
        for n, (src, c) in enumerate(((wo_own, core), (wo_other, 1 - core))):
            start = pl.multiple_of((2 * r + c) * shard, 16)
            loads_o.append(pltpu.make_async_copy(src.at[r], wo.at[pl.ds(start, shard), :], sems_o.at[n, r]))
    for t in range(tiles):
        at = slice(t * tile, t * tile + tile)
        loads_1.append(pltpu.make_async_copy(w1.at[:, at], w1v.at[:, at], sems_1.at[t]))
        loads_2.append(pltpu.make_async_copy(w2.at[at, :], w2v.at[at, :], sems_2.at[t]))
    for copy in loads_o:
        copy.start()
    for first, second in zip(loads_1, loads_2):
        first.start()
        second.start()
    for copy in loads_o:
        copy.wait()
    depth = 2 * shard
    total = tok[...].astype(F32) + out_bias[...]
    for r, att in enumerate((att0, att1, att2, att3)):
        total = total + jnp.dot(att[...], wo[r * depth : r * depth + depth, :], preferred_element_type=F32)
    after[...] = total
    h = norm(total, gain[...], bias[...]).astype(BF16)
    for t in range(tiles):
        at = slice(t * tile, t * tile + tile)
        loads_1[t].wait()
        pre = jnp.dot(h, w1v[:, at], preferred_element_type=F32) + b1[:, at]
        hidden = (0.5 * pre * (1.0 + lax.erf(pre * math.sqrt(0.5)))).astype(BF16)
        loads_2[t].wait()
        part = jnp.dot(hidden, w2v[at, :], preferred_element_type=F32)
        if t == 0:
            acc[...] = part
        else:
            acc[...] += part
    for place in range(4):

        @pl.when(me == place)
        def _(place=place):
            at = slice(place * quarter, place * quarter + quarter)
            mine[...] = acc[:, at] + after[:, at] + b2[:, at]
            for r, ref in ((1, to1), (2, to2), (3, to3)):
                first = (place ^ r) * quarter
                ref[...] = acc[:, first : first + quarter].astype(BF16)


def mlp(where, atts, tok, wo_own, wo_other, out_bias, gain, bias, w1, b1, w2, b2):
    rows, width = tok.shape
    groups, shard, _ = wo_own.shape
    hidden = w1.shape[1]
    quarter = width // 4
    tiles = 4
    return pl.pallas_call(
        mlp_kernel,
        in_specs=[SM, VM, VM, VM, VM, VM, ANY, ANY, VM, VM, VM, ANY, VM, ANY, VM],
        out_specs=[VM] * 4,
        out_shape=[jax.ShapeDtypeStruct((rows, quarter), F32)]
        + [jax.ShapeDtypeStruct((rows, quarter), BF16)] * 3,
        scratch_shapes=[
            pltpu.VMEM((2 * groups * shard, width), BF16),
            pltpu.VMEM(w1.shape, BF16),
            pltpu.VMEM(w2.shape, BF16),
            pltpu.VMEM((rows, width), F32),
            pltpu.VMEM((rows, width), F32),
            pltpu.SemaphoreType.DMA((2, groups)),
            pltpu.SemaphoreType.DMA((tiles,)),
            pltpu.SemaphoreType.DMA((tiles,)),
        ],
        compiler_params=params(),
        cost_estimate=cost(2 * rows * width * (width + 2 * hidden), 25e6, rows * hidden),
        name="out_mlp",
    )(where, *atts, tok, wo_own, wo_other, out_bias, gain, bias, w1, b1, w2, b2)


def project_kernel(where, layer, stats, gain, bias, wp_own, wp_other, mine, to1, to2, to3, wp, acc, sems):
    core, me = where[0], where[1]
    folds, shard, width = wp_own.shape
    quarter = mine.shape[1]
    count = mine.shape[0]
    copies = []
    for k in range(folds):
        for n, (src, c) in enumerate(((wp_own, core), (wp_other, 1 - core))):
            start = pl.multiple_of((2 * k + c) * shard, 16)
            copies.append(pltpu.make_async_copy(src.at[k], wp.at[pl.ds(start, shard), :], sems.at[n, k]))
    for copy in copies:
        copy.start()
    scale, shift = stats[:, 0:1], stats[:, 1:2]
    final = ((layer[...].astype(F32) - shift) * scale * gain[...] + bias[...]).astype(BF16)
    for copy in copies:
        copy.wait()
    depth = 2 * shard
    for k in range(folds):
        part = jnp.dot(
            final[k * count : k * count + count], wp[k * depth : k * depth + depth, :], preferred_element_type=F32
        )
        if k == 0:
            acc[...] = part
        else:
            acc[...] += part
    for place in range(4):

        @pl.when(me == place)
        def _(place=place):
            at = slice(place * quarter, place * quarter + quarter)
            mine[...] = acc[:, at]
            for r, ref in ((1, to1), (2, to2), (3, to3)):
                first = (place ^ r) * quarter
                ref[...] = acc[:, first : first + quarter].astype(BF16)


def project(where, layer, stats, gain, bias, wp_own, wp_other):
    folds, shard, width = wp_own.shape
    count = layer.shape[0] // folds
    quarter = width // 4
    return pl.pallas_call(
        project_kernel,
        in_specs=[SM, VM, VM, VM, VM, ANY, ANY],
        out_specs=[VM] * 4,
        out_shape=[jax.ShapeDtypeStruct((count, quarter), F32)]
        + [jax.ShapeDtypeStruct((count, quarter), BF16)] * 3,
        scratch_shapes=[
            pltpu.VMEM((2 * folds * shard, width), BF16),
            pltpu.VMEM((count, width), F32),
            pltpu.SemaphoreType.DMA((2, folds)),
        ],
        compiler_params=params(),
        cost_estimate=cost(2 * count * folds * 2 * shard * width, 7e6),
        name="project",
    )(where, layer, stats, gain, bias, wp_own, wp_other)


def gather_qkv(w_qkv, core):
    parts, shard, cols = w_qkv.shape
    count = lax.axis_size("tok")
    if shard % 16:
        whole = lax.all_gather(w_qkv, "tok", axis=1, tiled=True)
        low, high = whole[None, :, : whole.shape[1] // 2], whole[None, :, whole.shape[1] // 2 :]
        return jnp.where(core == 0, low, high), jnp.where(core == 0, high, low)
    own = lax.all_gather(
        w_qkv.reshape(parts * shard, cols), "tok", axis=0, tiled=True, axis_index_groups=same_core_groups(count)
    ).reshape(count // 2, parts, shard, cols)
    return own, swap(own, "tok", 1)


def gather_out(w_out, core, tok):
    depth, shard = w_out.shape
    count = lax.axis_size("tok")
    near = jnp.stack([w_out] + [swap(w_out, "tok", 2 * s) for s in range(1, count // 2)])
    far = swap(near, "tok", 1)
    slots = [(near if s % 2 == 0 else far)[s // 2] for s in range(count)]
    whole = jnp.concatenate(unxor(slots, tok), axis=1)
    half = depth // 2
    part = jnp.where(core == 0, whole[:half], whole[half:])
    own = gather_blk(part).reshape(4, half, whole.shape[1])
    return own, swap(own, "tok", 1)


def gather_proj(w_proj, core, blk):
    rows, quarter = w_proj.shape
    count = lax.axis_size("tok")
    width = 4 * quarter
    half = quarter // 2
    if rows == 2 * quarter and count == 8:
        halves = w_proj.reshape(2, 2, half, quarter)
        keep = jnp.where(core == 0, halves[:, 0], halves[:, 1])
        give = jnp.where(core == 0, halves[:, 1], halves[:, 0])
        got = swap(give, "tok", 1)
        low = jnp.where(core == 0, keep, got)
        high = jnp.where(core == 0, got, keep)
        pieces = unxor([low[0], low[1], high[0], high[1]], blk)
        pieces = [pieces[0]] + [swap(pieces[r], "blk", r) for r in range(1, 4)]
        mine = jnp.concatenate(unxor(pieces, blk), axis=1)
        own = lax.all_gather(mine, "tok", axis=0, tiled=True, axis_index_groups=same_core_groups(count))
        own = own.reshape(4, half, width)
        return own, swap(own, "tok", 1)
    whole = lax.all_gather(w_proj, "tok", axis=0, tiled=True).reshape(4, 4, quarter, quarter)
    whole = lax.all_to_all(whole, "blk", split_axis=1, concat_axis=3, tiled=True)
    whole = whole.reshape(4, 2, half, width)
    low, high = whole[:, 0], whole[:, 1]
    return jnp.where(core == 0, low, high), jnp.where(core == 0, high, low)


def body(
    tokens,
    segment_ids,
    merge_index,
    segment_owner,
    ln1_gain,
    ln1_bias,
    w_qkv,
    qkv_bias,
    w_out,
    out_bias,
    ln2_gain,
    ln2_bias,
    w_fc1,
    fc1_bias,
    w_fc2,
    fc2_bias,
    ln3_gain,
    ln3_bias,
    w_proj,
    proj_bias,
):
    blk, tok = lax.axis_index("blk"), lax.axis_index("tok")
    core = tok % 2
    tok_count = lax.axis_size("tok")
    where = jnp.stack([core, blk]).astype(jnp.int32)
    block = tokens[0]
    local_rows, width = block.shape
    rows = 4 * local_rows
    quarter = width // 4
    merges = merge_index[0]
    merged_count, folds = merges.shape

    gathered = gather_blk(block)
    qkv_own, qkv_other = gather_qkv(w_qkv, core)
    out_own, out_other = gather_out(w_out, core, tok)
    proj_own, proj_other = gather_proj(w_proj, core, blk)

    ids = jnp.arange(rows, dtype=jnp.int32)
    seg_of = jnp.sum(jnp.where(merges[:, :1] == ids[None, :], segment_ids[0][None, :], 0), axis=1)
    owners = segment_owner[0]
    owner = jnp.sum(
        jnp.where(seg_of[:, None] == jnp.arange(owners.shape[0], dtype=jnp.int32)[None, :], owners[None, :], 0),
        axis=1,
    )
    order = jnp.arange(merged_count, dtype=jnp.int32)
    ahead = (owner[None, :] < owner[:, None]) | ((owner[None, :] == owner[:, None]) & (order[None, :] < order[:, None]))
    place = jnp.sum(ahead.astype(jnp.int32), axis=1)
    at_place = place[None, :] == order[:, None]
    owner_sorted = jnp.sum(jnp.where(at_place, owner[None, :], 0), axis=1)
    merges_sorted = jnp.sum(jnp.where(at_place[:, :, None], merges[None, :, :], 0), axis=1)
    chunks = 2
    count = merged_count // chunks
    perm = merges_sorted.reshape(chunks, count, folds).transpose(0, 2, 1).reshape(rows, 1)
    row_owner = jnp.broadcast_to(owner_sorted.reshape(chunks, 1, count), (chunks, folds, count)).reshape(rows)
    source = ((ids // local_rows) ^ blk) * local_rows + ids % local_rows

    moved, normed = permute_norm(perm, source[None, :], gathered, ln1_gain[None, :], ln1_bias[None, :])
    qkv = qkv_project(where, normed, qkv_own, qkv_other, qkv_bias)

    chunk_rows = rows // chunks
    layers = []
    for n in range(chunks):
        at = slice(n * chunk_rows, n * chunk_rows + chunk_rows)
        att = attend(n * chunk_rows, chunk_rows, qkv, row_owner[at, None], row_owner[None, :])
        atts = [att] + [swap(att, "blk", r) for r in range(1, 4)]
        own, *sends = mlp(
            where, atts, moved[at], out_own, out_other, out_bias[None, :], ln2_gain[None, :], ln2_bias[None, :],
            w_fc1, fc1_bias[None, :], w_fc2, fc2_bias[None, :],
        )
        for r in range(1, 4):
            own = own + swap(sends[r - 1], "blk", r).astype(F32)
        layers.append(own.astype(BF16))

    gain3 = lax.dynamic_slice_in_dim(ln3_gain, blk * quarter, quarter, 0)
    bias3 = lax.dynamic_slice_in_dim(ln3_bias, blk * quarter, quarter, 0)
    outs = []
    for layer in layers:
        wide = layer.astype(F32)
        mean = jnp.mean(wide, axis=-1)
        centered = wide - mean[:, None]
        stat = jnp.stack([mean, jnp.sum(centered * centered, axis=-1)])
        stat = [stat] + [swap(stat, "blk", r) for r in range(1, 4)]
        means = [s[0] for s in stat]
        mean = sum(means) * 0.25
        spread = sum(s[1] for s in stat) + quarter * sum((m - mean) ** 2 for m in means)
        stats = jnp.stack([lax.rsqrt(spread / width + EPS), mean], axis=1)
        own, *sends = project(where, layer, stats, gain3[None, :], bias3[None, :], proj_own, proj_other)
        for r in range(1, 4):
            own = own + swap(sends[r - 1], "blk", r).astype(F32)
        outs.append((own + proj_bias[None, :]).astype(BF16))
    projected = jnp.concatenate(outs, axis=0)

    slot_cap = 2 * merged_count // tok_count
    first = jnp.sum((owner_sorted[None, :] < owner_sorted[:, None]).astype(jnp.int32), axis=1)
    target = owner_sorted * slot_cap + order - first
    placed = (jnp.arange(tok_count * slot_cap, dtype=jnp.int32)[:, None] == target[None, :]).astype(BF16)
    outgoing = jnp.dot(placed, projected, preferred_element_type=F32).astype(BF16)
    outgoing = outgoing.reshape(tok_count, slot_cap, projected.shape[1])
    arrived = lax.all_to_all(outgoing, "tok", split_axis=0, concat_axis=0, tiled=True)
    return arrived[None]


def solution(mesh):
    placed = (
        P("tok", "blk", None),
        P("tok", None),
        P("tok", None, None),
        P("tok", None),
        P(),
        P(),
        P(None, "tok", "blk"),
        P(None, "blk"),
        P("blk", "tok"),
        P(),
        P(),
        P(),
        P(None, "blk"),
        P("blk"),
        P("blk", None),
        P(),
        P(),
        P(),
        P("tok", "blk"),
        P("blk"),
    )
    return jax.shard_map(
        body, mesh=mesh, in_specs=placed, out_specs=P("tok", None, None, "blk"), check_vma=False
    )
```

time: 479 us -> 329 us (0.69)
  waiting for transfers between devices: 297 us -> 59.6 us
  Pallas kernels: 0 us -> 109 us
  matrix products: 70.2 us -> 0.35 us
  starting transfers between devices: 0.25 us -> 56.5 us
  other arithmetic: 24 us -> 12.7 us
    all_gather x5 -> x2, waiting for transfers between devices: 176 us -> 0.01 us  [the longest x1 0.01 us: gather_qkv(): lax.all_gather(w_qkv.reshape(parts * shard, cols), 'tok', axis=0, tiled=T...]
    pallas_call x0 -> x8, Pallas kernels: none -> 109 us  [the longest x2 55.3 us: mlp(): pl.pallas_call(mlp_kernel, in_specs=[SM, VM, VM, VM, VM, VM, ANY, ANY, VM...]
    psum x1 -> x0, waiting for transfers between devices: 75.4 us -> none  [body(): lax.psum(partial_sum.astype(jnp.bfloat16), 'blk').astype(jnp.float32)]
    dot_general x9 -> x1, matrix products: 70.2 us -> 0.35 us  [body(): jnp.dot(placed, projected, preferred_element_type=F32).astype(BF16)]
    ppermute x0 -> x47, waiting for transfers between devices: none -> 59.6 us  [swap(): lax.ppermute(x, axis, [(i, i ^ mask) for i in range(lax.axis_size(axis))])]
    ppermute x0 -> x47, starting transfers between devices: none -> 56.4 us  [swap(): lax.ppermute(x, axis, [(i, i ^ mask) for i in range(lax.axis_size(axis))])]
    reduce_scatter x1 -> x0, waiting for transfers between devices: 45.8 us -> none  [body(): lax.psum_scatter(jnp.dot(attended, out_full, preferred_element_type=jnp.f...]
    gather x3 -> x0, local copies, waits for them, and re-layouts: 12.6 us -> none  [the longest x2 11.3 us: body(): jnp.take(final_all, merge_rows.reshape(-1), axis=0)]
  transfers between devices with their start and end apart: 7 -> 49, of which waited for: 7 -> 19; matrix products, arithmetic and copies ran while one was open for 20% -> 17% of each run, Pallas kernels for 0% -> 32%
where the time goes in v1:
time: 329 us; the launch traced here: 325 us
  Pallas kernels  109 us (33%)
  waiting for transfers between devices  59.6 us (18%)
  starting transfers between devices  56.5 us (17%)
  local copies, waits for them, and re-layouts  48.9 us (15%)
  blocking collectives  24.3 us (7%)
  between operations  14.1 us (4%)
  other arithmetic  12.7 us (4%)
    ppermute x47, waiting for transfers between devices, swap(): lax.ppermute(x, axis, [(i, i ^ mask) for i in range(lax.axis_size(axis))])  59.6 us
    ppermute x47, starting transfers between devices, swap(): lax.ppermute(x, axis, [(i, i ^ mask) for i in range(lax.axis_size(axis))])  56.4 us
    pallas_call x2, Pallas kernels, mlp(): pl.pallas_call(mlp_kernel, in_specs=[SM, VM, VM, VM, VM, VM, ANY, ANY, VM...  55.3 us
    all_to_all x1, blocking collectives, body(): lax.all_to_all(outgoing, 'tok', split_axis=0, concat_axis=0, tiled=True)  24.3 us
    unnamed x65, local copies, waits for them, and re-layouts  23.4 us
    pallas_call x2, Pallas kernels, attend(): pl.pallas_call(functools.partial(attend_kernel, first, 256), in_specs=[VM...  18.4 us
    pallas_call x1, Pallas kernels, qkv_project(): pl.pallas_call(qkv_kernel, in_specs=[SM, VM, ANY, ANY, VM], out_specs=VM,...  13.8 us
    pallas_call x2, Pallas kernels, project(): pl.pallas_call(project_kernel, in_specs=[SM, VM, VM, VM, VM, ANY, ANY], o...  11.8 us
  transfers between devices with their start and end apart: 49, of which 19 were waited for; matrix products, arithmetic and copies ran while one was open for 17% of the time, Pallas kernels for 32%

profile of v1, /device:TPU:0, one launch (start us, length us, event | category | flops | bytes accessed | tf_op | source)
XLA Modules:
  0.0 325.3 jit_solution(11677447146454238693)
XLA Ops:
  6.5 5.0 %collective-permute-start.12 = (bf16[416,208]{1,0:T(8,128)(2,1)}, bf16[416,208]{1,0:T(8,128)(2,1)}, u32[]{:S(2)}, u32[]{:S(2)}) collective-permute-start(bf16[416,208]{1,0:T(8,128)(2,1)} %param.28), channel_id=1, source_target_pairs={{0,6},{1,7},{2,4},{3,5},{4,2},{5,3},{6,0},{7,1},{8,14},{9,15},{10,... | collective-permute-start | bytes 519176 | tf_op jit(solution)/shard_map/ppermute | solution.py:36
  12.2 2.1 slice_bitcast_fusion
  14.3 1.7 collective-permute-start
  16.0 2.1 copy.79
  20.2 1.5 copy.89
  21.8 1.3 copy.88
  26.0 4.1 %collective-permute-done.11 = bf16[416,208]{1,0:T(8,128)(2,1)} collective-permute-done((bf16[416,208]{1,0:T(8,128)(2,1)}, bf16[416,208]{1,0:T(8,128)(2,1)}, u32[]{:S(2)}, u32[]{:S(2)}) %collective-permute-start.11) | collective-permute-done | bytes 173088 | tf_op jit(solution)/shard_map/ppermute | solution.py:36
  30.1 1.3 pad_maximum_fusion
  37.6 1.3 dynamic_slice.6
  39.0 1.4 dynamic_slice.7
  42.4 1.5 collective-permute-start.29
  43.9 1.4 collective-permute-start.28
  45.9 1.3 broadcast_select_fusion.28
  49.6 1.6 collective-permute-start.14
  51.8 3.2 collective-permute-done.29
  54.9 1.5 collective-permute-start.2
  56.4 1.5 collective-permute-start.15
  61.0 3.2 collective-permute-done.14
  64.3 1.5 collective-permute-start.17
  65.8 1.7 constant_dynamic-update-slice_fusion.11
  67.5 3.3 %collective-permute-done.15 = bf16[104,1664]{1,0:T(8,128)(2,1)S(1)} collective-permute-done((bf16[104,1664]{1,0:T(8,128)(2,1)S(1)}, bf16[104,1664]{1,0:T(8,128)(2,1)S(1)}, u32[]{:S(2)}, u32[]{:S(2)}) %collective-permute-start.15) | collective-permute-done | bytes 346144 | tf_op jit(solution)/shard_map/ppermute | solution.py:36
  70.9 1.5 collective-permute-start.1
  73.1 2.1 collective-permute-done.16
  75.3 1.5 collective-permute-start.18
  76.8 6.0 %collective-permute-done.17 = bf16[104,1664]{1,0:T(8,128)(2,1)} collective-permute-done((bf16[104,1664]{1,0:T(8,128)(2,1)S(1)}, bf16[104,1664]{1,0:T(8,128)(2,1)}, u32[]{:S(2)}, u32[]{:S(2)}) %collective-permute-start.17) | collective-permute-done | bytes 346144 | tf_op jit(solution)/shard_map/ppermute | solution.py:36
  82.8 1.5 collective-permute-start.19
  85.0 1.7 constant_dynamic-update-slice_fusion.8
  86.8 2.9 copy.80
  89.8 2.0 constant_dynamic-update-slice_fusion.7
  91.7 1.5 collective-permute-start.3
  93.2 1.7 constant_dynamic-update-slice_fusion.6
  95.0 1.8 constant_dynamic-update-slice_fusion.5
  97.4 7.2 %collective-permute-done.3 = bf16[128,1664]{1,0:T(8,128)(2,1)S(1)} collective-permute-done((bf16[128,1664]{1,0:T(8,128)(2,1)}, bf16[128,1664]{1,0:T(8,128)(2,1)S(1)}, u32[]{:S(2)}, u32[]{:S(2)}) %collective-permute-start.3) | collective-permute-done | bytes 426016 | tf_op jit(solution)/shard_map/ppermute | solution.py:36
  107.6 5.4 %collective-permute-done.4 = bf16[128,1664]{1,0:T(8,128)(2,1)S(1)} collective-permute-done((bf16[128,1664]{1,0:T(8,128)(2,1)}, bf16[128,1664]{1,0:T(8,128)(2,1)S(1)}, u32[]{:S(2)}, u32[]{:S(2)}) %collective-permute-start.4) | collective-permute-done | bytes 426016 | tf_op jit(solution)/shard_map/ppermute | solution.py:36
  113.9 1.3 collective-permute-done.5
  116.0 9.5 %permute_norm.1 = (bf16[1024,1664]{1,0:T(8,128)(2,1)}, bf16[1024,1664]{1,0:T(8,128)(2,1)}) custom-call(s32[1024,1]{1,0:T(8,128)} %copy.78.perm, s32[1,1024]{1,0:T(1,128)} %fusion.10.place, bf16[1024,1664]{1,0:T(8,128)(2,1)} %constant_dynamic-update-slice_fusion.tok, f32[1,1664]{1,0:T(1,128)} %broadcast_in_dim.144.gain, f32[1,1664]{1,0:T(1,128)} %broadcast_in_dim.145.bias), custom_call_target="tpu_custom_call" | custom-call | flops 3489660928 | bytes 10223616 | tf_op jit(solution)/shard_map/permute_norm/pallas_call | solution.py:71
  125.5 1.4 copy-done.21
  126.9 13.8 %qkv_project.1.qkv = bf16[3,1024,416]{2,1,0:T(8,128)(2,1)} custom-call(s32[2]{0:T(128)} %pad_add_fusion.core.where, bf16[1024,1664]{1,0:T(8,128)(2,1)} %get-tuple-element.23.h, bf16[4,3,208,416]{3,2,1,0:T(8,128)(2,1)} %bitcast.192, bf16[4,3,208,416]{3,2,1,0:T(8,128)(2,1)} %copy-done.21, f32[3,416]{1,0:T(4,128)} %bias.1), custom_call_target="tpu_custom_call" | custom-call | flops 4253024256 | bytes 12000000 | tf_op jit(solution)/shard_map/qkv_project/pallas_call | solution.py:116
  141.3 9.1 %attend.2.att0 = bf16[512,416]{1,0:T(8,128)(2,1)} custom-call(bf16[3,1024,416]{2,1,0:T(8,128)(2,1)} %qkv_project.1.qkv, s32[512,1]{1,0:T(8,128)} %copy.81.row_owner, s32[1,1024]{1,0:T(1,128)} %bitcast.218), custom_call_target="tpu_custom_call" | custom-call | flops 872415232 | bytes 4000000 | tf_op jit(solution)/shard_map/attend/pallas_call | solution.py:153
  151.1 1.5 collective-permute-start.8
  152.6 1.3 collective-permute-start.9
  153.9 2.0 fusion.22
  155.9 9.2 %attend.3.att0 = bf16[512,416]{1,0:T(8,128)(2,1)} custom-call(bf16[3,1024,416]{2,1,0:T(8,128)(2,1)} %qkv_project.1.qkv, s32[512,1]{1,0:T(8,128)} %copy.85.row_owner, s32[1,1024]{1,0:T(1,128)} %bitcast.219), custom_call_target="tpu_custom_call" | custom-call | flops 872415232 | bytes 4000000 | tf_op jit(solution)/shard_map/attend/pallas_call | solution.py:153
  165.8 1.5 collective-permute-start.36
  167.4 3.7 %collective-permute-done.8.att2 = bf16[512,416]{1,0:T(8,128)(2,1)} collective-permute-done((bf16[512,416]{1,0:T(8,128)(2,1)}, bf16[512,416]{1,0:T(8,128)(2,1)}, u32[]{:S(2)}, u32[]{:S(2)}) %collective-permute-start.8) | collective-permute-done | bytes 426016 | tf_op jit(solution)/shard_map/ppermute | solution.py:36
  171.1 5.8 %collective-permute-start.37 = (bf16[512,416]{1,0:T(8,128)(2,1)}, bf16[512,416]{1,0:T(8,128)(2,1)S(1)}, u32[]{:S(2)}, u32[]{:S(2)}) collective-permute-start(bf16[512,416]{1,0:T(8,128)(2,1)} %attend.3.att0), channel_id=1, source_target_pairs={{0,24},{8,16},{16,8},{24,0},{1,25},{9,17},{17,9},{25,1},{2,26},{10... | collective-permute-start | bytes 1277960 | tf_op jit(solution)/shard_map/ppermute | solution.py:36
  177.8 27.6 %out_mlp.2 = (f32[512,416]{1,0:T(8,128)}, bf16[512,416]{1,0:T(8,128)(2,1)}, bf16[512,416]{1,0:T(8,128)(2,1)}, bf16[512,416]{1,0:T(8,128)(2,1)}) custom-call(s32[2]{0:T(128)} %pad_add_fusion.core.where, bf16[512,416]{1,0:T(8,128)(2,1)} %attend.2.att0, bf16[512,416]{1,0:T(8,128)(2,1)} %collective-permute-done.7.att1, ...), custom_call_target="tpu_custom_call" | custom-call | flops 9814671360 | bytes 25000000 | tf_op jit(solution)/shard_map/out_mlp/pallas_call | solution.py:224
  206.2 1.5 collective-permute-start.22
  207.7 1.4 collective-permute-start.21
  209.8 27.8 %out_mlp.3 = (f32[512,416]{1,0:T(8,128)}, bf16[512,416]{1,0:T(8,128)(2,1)}, bf16[512,416]{1,0:T(8,128)(2,1)}, bf16[512,416]{1,0:T(8,128)(2,1)}) custom-call(s32[2]{0:T(128)} %pad_add_fusion.core.where, bf16[512,416]{1,0:T(8,128)(2,1)} %attend.3.att0, bf16[512,416]{1,0:T(8,128)(2,1)} %copy-done.22, bf16[512,416]{1,0:T(8,128)(2,1)} %copy-done.23, ...), custom_call_target="tpu_custom_call" | custom-call | flops 9814671360 | bytes 25000000 | tf_op jit(solution)/shard_map/out_mlp/pallas_call | solution.py:224
  238.3 1.5 collective-permute-start.39
  239.8 1.4 collective-permute-start.38
  241.2 1.4 convert_reduce_fusion.1
  243.6 8.5 %collective-permute-done.40 = bf16[512,416]{1,0:T(8,128)(2,1)S(1)} collective-permute-done((bf16[512,416]{1,0:T(8,128)(2,1)}, bf16[512,416]{1,0:T(8,128)(2,1)S(1)}, u32[]{:S(2)}, u32[]{:S(2)}) %collective-permute-start.40) | collective-permute-done | bytes 426016 | tf_op jit(solution)/shard_map/ppermute | solution.py:36
  252.5 4.4 %collective-permute-done.39 = bf16[512,416]{1,0:T(8,128)(2,1)S(1)} collective-permute-done((bf16[512,416]{1,0:T(8,128)(2,1)}, bf16[512,416]{1,0:T(8,128)(2,1)S(1)}, u32[]{:S(2)}, u32[]{:S(2)}) %collective-permute-start.39) | collective-permute-done | bytes 426016 | tf_op jit(solution)/shard_map/ppermute | solution.py:36
  259.7 1.4 collective-permute-start.43
  265.7 1.5 copy-done
  267.2 5.9 %project.2 = (f32[128,416]{1,0:T(8,128)}, bf16[128,416]{1,0:T(8,128)(2,1)}, bf16[128,416]{1,0:T(8,128)(2,1)}, bf16[128,416]{1,0:T(8,128)(2,1)}) custom-call(s32[2]{0:T(128)} %pad_add_fusion.core.where, bf16[512,416]{1,0:T(8,128)(2,1)} %copy-done.1, f32[512,2]{1,0:T(8,128)} %copy.84.stats, f32[1,416]{1,0:T(1,128)} %bitcast.205, f32[1,416]{1,0:T(1,128)} %bitcast.207, ...), custom_call_target="tpu_custom_call" | custom-call | flops 708837376 | bytes 7000000 | tf_op jit(solution)/shard_map/project/pallas_call | solution.py:286
  275.2 1.5 collective-permute-start.33
  277.5 5.9 %project.3 = (f32[128,416]{1,0:T(8,128)}, bf16[128,416]{1,0:T(8,128)(2,1)}, bf16[128,416]{1,0:T(8,128)(2,1)}, bf16[128,416]{1,0:T(8,128)(2,1)}) custom-call(s32[2]{0:T(128)} %pad_add_fusion.core.where, bf16[512,416]{1,0:T(8,128)(2,1)} %copy-done.2, f32[512,2]{1,0:T(8,128)} %copy.86.stats, f32[1,416]{1,0:T(1,128)} %bitcast.206, f32[1,416]{1,0:T(1,128)} %bitcast.208, ...), custom_call_target="tpu_custom_call" | custom-call | flops 708837376 | bytes 7000000 | tf_op jit(solution)/shard_map/project/pallas_call | solution.py:286
  283.4 1.3 collective-permute-start.46
  284.8 1.5 collective-permute-start.45
  287.0 2.7 collective-permute-done.46
  293.1 24.3 %all_to_all.5 = bf16[8,64,416]{2,1,0:T(8,128)(2,1)S(1)} all-to-all(bf16[8,64,416]{2,1,0:T(8,128)(2,1)S(1)} %bitcast.193), channel_id=1, replica_groups=mesh['blk'=4,'tok'=8] {'tok'}, dimensions={0} | all-to-all | bytes 851968 | tf_op jit(solution)/shard_map/all_to_all | solution.py:453
  (171 shorter events, 48.9 us)
Async XLA Ops:
  6.5 11.7 %copy-start.9 = (bf16[832,416]{0,1:T(8,128)(2,1)S(1)}, bf16[832,416]{0,1:T(8,128)(2,1)}, u32[]{:S(2)}) copy-start(bf16[832,416]{0,1:T(8,128)(2,1)} %param.38) | copy-start | bytes 2076676
  6.5 80.2 %all-gather.6.cloned.1.call-start = ((), (), s32[]{:S(2)}) async-start(), calls=%async_computation.2 | async-start | bytes 2662400 | tf_op jit(solution)/shard_map/all_gather | solution.py:310
  6.5 19.4 %collective-permute-start.12 = (bf16[416,208]{1,0:T(8,128)(2,1)}, bf16[416,208]{1,0:T(8,128)(2,1)}, u32[]{:S(2)}, u32[]{:S(2)}) collective-permute-start(bf16[416,208]{1,0:T(8,128)(2,1)} %param.28), channel_id=1, source_target_pairs={{0,6},{1,7},{2,4},{3,5},{4,2},{5,3},{6,0},{7,1},{8,14},{9,15},{10,... | collective-permute-start | bytes 519176 | tf_op jit(solution)/shard_map/ppermute | solution.py:36
  11.6 18.5 %collective-permute-start.11 = (bf16[416,208]{1,0:T(8,128)(2,1)}, bf16[416,208]{1,0:T(8,128)(2,1)}, u32[]{:S(2)}, u32[]{:S(2)}) collective-permute-start(bf16[416,208]{1,0:T(8,128)(2,1)} %param.28), channel_id=1, source_target_pairs={{0,4},{1,5},{2,6},{3,7},{4,0},{5,1},{6,2},{7,3},{8,12},{9,13},{10,... | collective-permute-start | bytes 519176 | tf_op jit(solution)/shard_map/ppermute | solution.py:36
  11.6 18.5 %collective-permute-start.10 = (bf16[416,208]{1,0:T(8,128)(2,1)}, bf16[416,208]{1,0:T(8,128)(2,1)}, u32[]{:S(2)}, u32[]{:S(2)}) collective-permute-start(bf16[416,208]{1,0:T(8,128)(2,1)} %param.28), channel_id=1, source_target_pairs={{0,2},{1,3},{2,0},{3,1},{4,6},{5,7},{6,4},{7,5},{8,10},{9,11},{10,... | collective-permute-start | bytes 519176 | tf_op jit(solution)/shard_map/ppermute | solution.py:36
  14.3 80.7 %collective-permute-start = (bf16[128,1664]{1,0:T(8,128)(2,1)}, bf16[128,1664]{1,0:T(8,128)(2,1)}, u32[]{:S(2)}, u32[]{:S(2)}) collective-permute-start(bf16[128,1664]{1,0:T(8,128)(2,1)} %get-tuple-element.88), channel_id=1, source_target_pairs={{0,8},{8,0},{16,24},{24,16},{1,9},{9,1},{17,25},{25,17},{2,10},{10... | collective-permute-start | bytes 1277960 | tf_op jit(solution)/shard_map/ppermute | solution.py:36
  18.1 137.8 %all-gather.4.cloned.1.call-start = ((), (), s32[]{:S(2)}) async-start(), calls=%async_computation.1 | async-start | bytes 3461120 | tf_op jit(solution)/shard_map/all_gather | solution.py:344
  21.8 8.3 %copy-start.8 = (bf16[416,208]{1,0:T(8,128)(2,1)S(1)}, bf16[416,208]{1,0:T(8,128)(2,1)}, u32[]{:S(2)}) copy-start(bf16[416,208]{1,0:T(8,128)(2,1)} %param.28) | copy-start | bytes 519172
  23.1 10.1 %copy-start.11 = (f32[1664]{0:T(1024)S(1)}, f32[1664]{0:T(1024)}, u32[]{:S(2)}) copy-start(f32[1664]{0:T(1024)} %param.24) | copy-start | bytes 19972
  23.1 10.6 %copy-start.12 = (f32[1664]{0:T(1024)S(1)}, f32[1664]{0:T(1024)}, u32[]{:S(2)}) copy-start(f32[1664]{0:T(1024)} %param.25) | copy-start | bytes 19972
  23.1 12.1 %copy-start.13 = (f32[1664]{0:T(1024)S(1)}, f32[1664]{0:T(1024)}, u32[]{:S(2)}) copy-start(f32[1664]{0:T(1024)} %param.29) | copy-start | bytes 19972
  23.1 12.7 %copy-start.14 = (f32[1664]{0:T(1024)S(1)}, f32[1664]{0:T(1024)}, u32[]{:S(2)}) copy-start(f32[1664]{0:T(1024)} %param.30) | copy-start | bytes 19972
  23.1 13.3 %copy-start.15 = (f32[1664]{0:T(1024)S(1)}, f32[1664]{0:T(1024)}, u32[]{:S(2)}) copy-start(f32[1664]{0:T(1024)} %param.31) | copy-start | bytes 19972
  23.2 13.9 %copy-start.16 = (f32[1664]{0:T(1024)S(1)}, f32[1664]{0:T(1024)}, u32[]{:S(2)}) copy-start(f32[1664]{0:T(1024)} %param.35) | copy-start | bytes 19972
  24.0 17.4 %collective-permute-start.27 = (bf16[2,208,416]{2,1,0:T(8,128)(2,1)}, bf16[2,208,416]{2,1,0:T(8,128)(2,1)S(1)}, u32[]{:S(2)}, u32[]{:S(2)}) collective-permute-start(bf16[2,208,416]{2,1,0:T(8,128)(2,1)} %select_bitcast_fusion), channel_id=1, source_target_pairs={{0,1},{1,0},{2,3},{3,2},{4,5},{5,4},{6,7},{7,6},{8,9},{9,8},{10,11... | collective-permute-start | bytes 1038344 | tf_op jit(solution)/shard_map/ppermute | solution.py:36
  31.4 14.4 %collective-permute-start.13 = (bf16[4,416,208]{2,1,0:T(8,128)(2,1)S(1)}, bf16[4,416,208]{2,1,0:T(8,128)(2,1)S(1)}, u32[]{:S(2)}, u32[]{:S(2)}) collective-permute-start(bf16[4,416,208]{2,1,0:T(8,128)(2,1)S(1)} %pad_maximum_fusion), channel_id=1, source_target_pairs={{0,1},{1,0},{2,3},{3,2},{4,5},{5,4},{6,7},{7,6},{8,9},{9,8},{10,11... | collective-permute-start | bytes 2076680 | tf_op jit(solution)/shard_map/ppermute | solution.py:36
  42.4 12.5 %collective-permute-start.29 = (bf16[208,416]{1,0:T(8,128)(2,1)}, bf16[208,416]{1,0:T(8,128)(2,1)}, u32[]{:S(2)}, u32[]{:S(2)}) collective-permute-start(bf16[208,416]{1,0:T(8,128)(2,1)} %get-tuple-element.45), channel_id=1, source_target_pairs={{0,16},{8,24},{16,0},{24,8},{1,17},{9,25},{17,1},{25,9},{2,18},{10... | collective-permute-start | bytes 519176 | tf_op jit(solution)/shard_map/ppermute | solution.py:36
  43.9 12.5 %collective-permute-start.28 = (bf16[208,416]{1,0:T(8,128)(2,1)}, bf16[208,416]{1,0:T(8,128)(2,1)}, u32[]{:S(2)}, u32[]{:S(2)}) collective-permute-start(bf16[208,416]{1,0:T(8,128)(2,1)} %get-tuple-element.78), channel_id=1, source_target_pairs={{0,24},{8,16},{16,8},{24,0},{1,25},{9,17},{17,9},{25,1},{2,26},{10... | collective-permute-start | bytes 519176 | tf_op jit(solution)/shard_map/ppermute | solution.py:36
  45.3 12.6 %collective-permute-start.30 = (bf16[208,416]{1,0:T(8,128)(2,1)}, bf16[208,416]{1,0:T(8,128)(2,1)}, u32[]{:S(2)}, u32[]{:S(2)}) collective-permute-start(bf16[208,416]{1,0:T(8,128)(2,1)} %get-tuple-element.77), channel_id=1, source_target_pairs={{0,8},{8,0},{16,24},{24,16},{1,9},{9,1},{17,25},{25,17},{2,10},{10... | collective-permute-start | bytes 519176 | tf_op jit(solution)/shard_map/ppermute | solution.py:36
  49.6 14.7 %collective-permute-start.14 = (bf16[104,1664]{1,0:T(8,128)(2,1)S(1)}, bf16[104,1664]{1,0:T(8,128)(2,1)}, u32[]{:S(2)}, u32[]{:S(2)}) collective-permute-start(bf16[104,1664]{1,0:T(8,128)(2,1)S(1)} %get-tuple-element.90), channel_id=1, source_target_pairs={{0,8},{8,0},{16,24},{24,16},{1,9},{9,1},{17,25},{25,17},{2,10},{10... | collective-permute-start | bytes 1038344 | tf_op jit(solution)/shard_map/ppermute | solution.py:36
  54.9 51.1 %collective-permute-start.2 = (bf16[128,1664]{1,0:T(8,128)(2,1)}, bf16[128,1664]{1,0:T(8,128)(2,1)S(1)}, u32[]{:S(2)}, u32[]{:S(2)}) collective-permute-start(bf16[128,1664]{1,0:T(8,128)(2,1)} %get-tuple-element.88), channel_id=1, source_target_pairs={{0,16},{8,24},{16,0},{24,8},{1,17},{9,25},{17,1},{25,9},{2,18},{10... | collective-permute-start | bytes 1277960 | tf_op jit(solution)/shard_map/ppermute | solution.py:36
  56.4 14.4 %collective-permute-start.15 = (bf16[104,1664]{1,0:T(8,128)(2,1)S(1)}, bf16[104,1664]{1,0:T(8,128)(2,1)S(1)}, u32[]{:S(2)}, u32[]{:S(2)}) collective-permute-start(bf16[104,1664]{1,0:T(8,128)(2,1)S(1)} %get-tuple-element.89), channel_id=1, source_target_pairs={{0,8},{8,0},{16,24},{24,16},{1,9},{9,1},{17,25},{25,17},{2,10},{10... | collective-permute-start | bytes 1038344 | tf_op jit(solution)/shard_map/ppermute | solution.py:36
  60.5 14.8 %collective-permute-start.16 = (bf16[104,1664]{1,0:T(8,128)(2,1)S(1)}, bf16[104,1664]{1,0:T(8,128)(2,1)S(1)}, u32[]{:S(2)}, u32[]{:S(2)}) collective-permute-start(bf16[104,1664]{1,0:T(8,128)(2,1)S(1)} %get-tuple-element.90), channel_id=1, source_target_pairs={{0,16},{8,24},{16,0},{24,8},{1,17},{9,25},{17,1},{25,9},{2,18},{10... | collective-permute-start | bytes 1038344 | tf_op jit(solution)/shard_map/ppermute | solution.py:36
  64.3 18.5 %collective-permute-start.17 = (bf16[104,1664]{1,0:T(8,128)(2,1)S(1)}, bf16[104,1664]{1,0:T(8,128)(2,1)}, u32[]{:S(2)}, u32[]{:S(2)}) collective-permute-start(bf16[104,1664]{1,0:T(8,128)(2,1)S(1)} %get-tuple-element.89), channel_id=1, source_target_pairs={{0,16},{8,24},{16,0},{24,8},{1,17},{9,25},{17,1},{25,9},{2,18},{10... | collective-permute-start | bytes 1038344 | tf_op jit(solution)/shard_map/ppermute | solution.py:36
  70.9 26.0 %collective-permute-start.1 = (bf16[128,1664]{1,0:T(8,128)(2,1)}, bf16[128,1664]{1,0:T(8,128)(2,1)S(1)}, u32[]{:S(2)}, u32[]{:S(2)}) collective-permute-start(bf16[128,1664]{1,0:T(8,128)(2,1)} %get-tuple-element.87), channel_id=1, source_target_pairs={{0,8},{8,0},{16,24},{24,16},{1,9},{9,1},{17,25},{25,17},{2,10},{10... | collective-permute-start | bytes 1277960 | tf_op jit(solution)/shard_map/ppermute | solution.py:36
  75.3 14.4 %collective-permute-start.18 = (bf16[104,1664]{1,0:T(8,128)(2,1)}, bf16[104,1664]{1,0:T(8,128)(2,1)}, u32[]{:S(2)}, u32[]{:S(2)}) collective-permute-start(bf16[104,1664]{1,0:T(8,128)(2,1)} %collective-permute-done.14), channel_id=1, source_target_pairs={{0,16},{8,24},{16,0},{24,8},{1,17},{9,25},{17,1},{25,9},{2,18},{10... | collective-permute-start | bytes 1038344 | tf_op jit(solution)/shard_map/ppermute | solution.py:36
  82.8 8.9 %collective-permute-start.19 = (bf16[104,1664]{1,0:T(8,128)(2,1)}, bf16[104,1664]{1,0:T(8,128)(2,1)}, u32[]{:S(2)}, u32[]{:S(2)}) collective-permute-start(bf16[104,1664]{1,0:T(8,128)(2,1)} %collective-permute-done.17), channel_id=1, source_target_pairs={{0,8},{8,0},{16,24},{24,16},{1,9},{9,1},{17,25},{25,17},{2,10},{10... | collective-permute-start | bytes 1038344 | tf_op jit(solution)/shard_map/ppermute | solution.py:36
  89.7 24.2 %copy-start.5 = (bf16[4,624,416]{2,1,0:T(8,128)(2,1)}, bf16[4,624,416]{2,1,0:T(8,128)(2,1)S(1)}, u32[]{:S(2)}) copy-start(bf16[4,624,416]{2,1,0:T(8,128)(2,1)S(1)} %copy.80) | copy-start | bytes 6230020
  89.7 35.8 %collective-permute-start.6 = (bf16[4,3,208,416]{3,2,1,0:T(8,128)(2,1)S(1)}, bf16[4,3,208,416]{3,2,1,0:T(8,128)(2,1)S(1)}, u32[]{:S(2)}, u32[]{:S(2)}) collective-permute-start(bf16[4,3,208,416]{3,2,1,0:T(8,128)(2,1)S(1)} %bitcast.191), channel_id=1, source_target_pairs={{0,1},{1,0},{2,3},{3,2},{4,5},{5,4},{6,7},{7,6},{8,9},{9,8},{10,11... | collective-permute-start | bytes 6230024 | tf_op jit(solution)/shard_map/ppermute | solution.py:36
  91.7 12.9 %collective-permute-start.3 = (bf16[128,1664]{1,0:T(8,128)(2,1)}, bf16[128,1664]{1,0:T(8,128)(2,1)S(1)}, u32[]{:S(2)}, u32[]{:S(2)}) collective-permute-start(bf16[128,1664]{1,0:T(8,128)(2,1)} %get-tuple-element.87), channel_id=1, source_target_pairs={{0,16},{8,24},{16,0},{24,8},{1,17},{9,25},{17,1},{25,9},{2,18},{10... | collective-permute-start | bytes 1277960 | tf_op jit(solution)/shard_map/ppermute | solution.py:36
  95.0 70.2 %collective-permute-start.20 = (bf16[4,208,1664]{2,1,0:T(8,128)(2,1)}, bf16[4,208,1664]{2,1,0:T(8,128)(2,1)}, u32[]{:S(2)}, u32[]{:S(2)}) collective-permute-start(bf16[4,208,1664]{2,1,0:T(8,128)(2,1)} %bitcast.197), channel_id=1, source_target_pairs={{0,1},{1,0},{2,3},{3,2},{4,5},{5,4},{6,7},{7,6},{8,9},{9,8},{10,11... | collective-permute-start | bytes 8306696 | tf_op jit(solution)/shard_map/ppermute | solution.py:36
  96.8 16.2 %collective-permute-start.4 = (bf16[128,1664]{1,0:T(8,128)(2,1)}, bf16[128,1664]{1,0:T(8,128)(2,1)S(1)}, u32[]{:S(2)}, u32[]{:S(2)}) collective-permute-start(bf16[128,1664]{1,0:T(8,128)(2,1)} %collective-permute-done), channel_id=1, source_target_pairs={{0,16},{8,24},{16,0},{24,8},{1,17},{9,25},{17,1},{25,9},{2,18},{10... | collective-permute-start | bytes 1277960 | tf_op jit(solution)/shard_map/ppermute | solution.py:36
  104.6 10.6 %collective-permute-start.5 = (bf16[128,1664]{1,0:T(8,128)(2,1)S(1)}, bf16[128,1664]{1,0:T(8,128)(2,1)S(1)}, u32[]{:S(2)}, u32[]{:S(2)}) collective-permute-start(bf16[128,1664]{1,0:T(8,128)(2,1)S(1)} %collective-permute-done.3), channel_id=1, source_target_pairs={{0,8},{8,0},{16,24},{24,16},{1,9},{9,1},{17,25},{25,17},{2,10},{10... | collective-permute-start | bytes 1277960 | tf_op jit(solution)/shard_map/ppermute | solution.py:36
  140.7 13.2 %copy-start.3 = (bf16[1024,1664]{1,0:T(8,128)(2,1)S(1)}, bf16[1024,1664]{1,0:T(8,128)(2,1)}, u32[]{:S(2)}) copy-start(bf16[1024,1664]{1,0:T(8,128)(2,1)} %get-tuple-element.24) | copy-start | bytes 10223620
  150.5 15.4 %collective-permute-start.7 = (bf16[512,416]{1,0:T(8,128)(2,1)}, bf16[512,416]{1,0:T(8,128)(2,1)}, u32[]{:S(2)}, u32[]{:S(2)}) collective-permute-start(bf16[512,416]{1,0:T(8,128)(2,1)} %attend.2.att0), channel_id=1, source_target_pairs={{0,8},{8,0},{16,24},{24,16},{1,9},{9,1},{17,25},{25,17},{2,10},{10... | collective-permute-start | bytes 1277960 | tf_op jit(solution)/shard_map/ppermute | solution.py:36
  151.1 20.0 %collective-permute-start.8 = (bf16[512,416]{1,0:T(8,128)(2,1)}, bf16[512,416]{1,0:T(8,128)(2,1)}, u32[]{:S(2)}, u32[]{:S(2)}) collective-permute-start(bf16[512,416]{1,0:T(8,128)(2,1)} %attend.2.att0), channel_id=1, source_target_pairs={{0,16},{8,24},{16,0},{24,8},{1,17},{9,25},{17,1},{25,9},{2,18},{10... | collective-permute-start | bytes 1277960 | tf_op jit(solution)/shard_map/ppermute | solution.py:36
  152.6 25.2 %collective-permute-start.9 = (bf16[512,416]{1,0:T(8,128)(2,1)}, bf16[512,416]{1,0:T(8,128)(2,1)}, u32[]{:S(2)}, u32[]{:S(2)}) collective-permute-start(bf16[512,416]{1,0:T(8,128)(2,1)} %attend.2.att0), channel_id=1, source_target_pairs={{0,24},{8,16},{16,8},{24,0},{1,25},{9,17},{17,9},{25,1},{2,26},{10... | collective-permute-start | bytes 1277960 | tf_op jit(solution)/shard_map/ppermute | solution.py:36
  155.9 109.7 %collective-permute-start.31 = (bf16[4,208,1664]{2,1,0:T(8,128)(2,1)}, bf16[4,208,1664]{2,1,0:T(8,128)(2,1)S(1)}, u32[]{:S(2)}, u32[]{:S(2)}) collective-permute-start(bf16[4,208,1664]{2,1,0:T(8,128)(2,1)} %bitcast.188), channel_id=1, source_target_pairs={{0,1},{1,0},{2,3},{3,2},{4,5},{5,4},{6,7},{7,6},{8,9},{9,8},{10,11... | collective-permute-start | bytes 8306696 | tf_op jit(solution)/shard_map/ppermute | solution.py:36
  165.2 41.0 %collective-permute-start.35 = (bf16[512,416]{1,0:T(8,128)(2,1)}, bf16[512,416]{1,0:T(8,128)(2,1)S(1)}, u32[]{:S(2)}, u32[]{:S(2)}) collective-permute-start(bf16[512,416]{1,0:T(8,128)(2,1)} %attend.3.att0), channel_id=1, source_target_pairs={{0,8},{8,0},{16,24},{24,16},{1,9},{9,1},{17,25},{25,17},{2,10},{10... | collective-permute-start | bytes 1277960 | tf_op jit(solution)/shard_map/ppermute | solution.py:36
  165.8 41.8 %collective-permute-start.36 = (bf16[512,416]{1,0:T(8,128)(2,1)}, bf16[512,416]{1,0:T(8,128)(2,1)S(1)}, u32[]{:S(2)}, u32[]{:S(2)}) collective-permute-start(bf16[512,416]{1,0:T(8,128)(2,1)} %attend.3.att0), channel_id=1, source_target_pairs={{0,16},{8,24},{16,0},{24,8},{1,17},{9,25},{17,1},{25,9},{2,18},{10... | collective-permute-start | bytes 1277960 | tf_op jit(solution)/shard_map/ppermute | solution.py:36
  171.1 37.9 %collective-permute-start.37 = (bf16[512,416]{1,0:T(8,128)(2,1)}, bf16[512,416]{1,0:T(8,128)(2,1)S(1)}, u32[]{:S(2)}, u32[]{:S(2)}) collective-permute-start(bf16[512,416]{1,0:T(8,128)(2,1)} %attend.3.att0), channel_id=1, source_target_pairs={{0,24},{8,16},{16,8},{24,0},{1,25},{9,17},{17,9},{25,1},{2,26},{10... | collective-permute-start | bytes 1277960 | tf_op jit(solution)/shard_map/ppermute | solution.py:36
  205.4 32.8 %collective-permute-start.23 = (bf16[512,416]{1,0:T(8,128)(2,1)}, bf16[512,416]{1,0:T(8,128)(2,1)S(1)}, u32[]{:S(2)}, u32[]{:S(2)}) collective-permute-start(bf16[512,416]{1,0:T(8,128)(2,1)} %get-tuple-element.28), channel_id=1, source_target_pairs={{0,24},{8,16},{16,8},{24,0},{1,25},{9,17},{17,9},{25,1},{2,26},{10... | collective-permute-start | bytes 1277960 | tf_op jit(solution)/shard_map/ppermute | solution.py:36
  206.2 33.6 %collective-permute-start.22 = (bf16[512,416]{1,0:T(8,128)(2,1)}, bf16[512,416]{1,0:T(8,128)(2,1)S(1)}, u32[]{:S(2)}, u32[]{:S(2)}) collective-permute-start(bf16[512,416]{1,0:T(8,128)(2,1)} %get-tuple-element.27), channel_id=1, source_target_pairs={{0,16},{8,24},{16,0},{24,8},{1,17},{9,25},{17,1},{25,9},{2,18},{10... | collective-permute-start | bytes 1277960 | tf_op jit(solution)/shard_map/ppermute | solution.py:36
  207.7 33.5 %collective-permute-start.21 = (bf16[512,416]{1,0:T(8,128)(2,1)}, bf16[512,416]{1,0:T(8,128)(2,1)}, u32[]{:S(2)}, u32[]{:S(2)}) collective-permute-start(bf16[512,416]{1,0:T(8,128)(2,1)} %get-tuple-element.26), channel_id=1, source_target_pairs={{0,8},{8,0},{16,24},{24,16},{1,9},{9,1},{17,25},{25,17},{2,10},{10... | collective-permute-start | bytes 1277960 | tf_op jit(solution)/shard_map/ppermute | solution.py:36
  209.8 31.3 %copy-start.7 = (f32[512,416]{1,0:T(8,128)S(1)}, f32[512,416]{1,0:T(8,128)}, u32[]{:S(2)}) copy-start(f32[512,416]{1,0:T(8,128)} %get-tuple-element.25) | copy-start | bytes 2555908
  237.6 20.6 %copy-start.6 = (f32[512,416]{1,0:T(8,128)S(1)}, f32[512,416]{1,0:T(8,128)}, u32[]{:S(2)}) copy-start(f32[512,416]{1,0:T(8,128)} %get-tuple-element.33) | copy-start | bytes 2555908
  237.6 14.4 %collective-permute-start.40 = (bf16[512,416]{1,0:T(8,128)(2,1)}, bf16[512,416]{1,0:T(8,128)(2,1)S(1)}, u32[]{:S(2)}, u32[]{:S(2)}) collective-permute-start(bf16[512,416]{1,0:T(8,128)(2,1)} %get-tuple-element.36), channel_id=1, source_target_pairs={{0,24},{8,16},{16,8},{24,0},{1,25},{9,17},{17,9},{25,1},{2,26},{10... | collective-permute-start | bytes 1277960 | tf_op jit(solution)/shard_map/ppermute | solution.py:36
  238.3 18.7 %collective-permute-start.39 = (bf16[512,416]{1,0:T(8,128)(2,1)}, bf16[512,416]{1,0:T(8,128)(2,1)S(1)}, u32[]{:S(2)}, u32[]{:S(2)}) collective-permute-start(bf16[512,416]{1,0:T(8,128)(2,1)} %get-tuple-element.35), channel_id=1, source_target_pairs={{0,16},{8,24},{16,0},{24,8},{1,17},{9,25},{17,1},{25,9},{2,18},{10... | collective-permute-start | bytes 1277960 | tf_op jit(solution)/shard_map/ppermute | solution.py:36
  239.8 18.4 %collective-permute-start.38 = (bf16[512,416]{1,0:T(8,128)(2,1)}, bf16[512,416]{1,0:T(8,128)(2,1)S(1)}, u32[]{:S(2)}, u32[]{:S(2)}) collective-permute-start(bf16[512,416]{1,0:T(8,128)(2,1)} %get-tuple-element.34), channel_id=1, source_target_pairs={{0,8},{8,0},{16,24},{24,16},{1,9},{9,1},{17,25},{25,17},{2,10},{10... | collective-permute-start | bytes 1277960 | tf_op jit(solution)/shard_map/ppermute | solution.py:36
  242.5 23.1 %copy-start.1 = (bf16[512,416]{1,0:T(8,128)(2,1)}, bf16[512,416]{1,0:T(8,128)(2,1)S(1)}, u32[]{:S(2)}) copy-start(bf16[512,416]{1,0:T(8,128)(2,1)S(1)} %get-tuple-element.44.layer) | copy-start | bytes 1277956
  242.9 18.2 %collective-permute-start.26 = (f32[2,512]{1,0:T(2,128)S(1)}, f32[2,512]{1,0:T(2,128)S(1)}, u32[]{:S(2)}, u32[]{:S(2)}) collective-permute-start(f32[2,512]{1,0:T(2,128)S(1)} %pad_maximum_fusion.1), channel_id=1, source_target_pairs={{0,24},{8,16},{16,8},{24,0},{1,25},{9,17},{17,9},{25,1},{2,26},{10... | collective-permute-start | bytes 12296 | tf_op jit(solution)/shard_map/ppermute | solution.py:36
  252.0 10.0 %collective-permute-start.25 = (f32[2,512]{1,0:T(2,128)S(1)}, f32[2,512]{1,0:T(2,128)S(1)}, u32[]{:S(2)}, u32[]{:S(2)}) collective-permute-start(f32[2,512]{1,0:T(2,128)S(1)} %pad_maximum_fusion.1), channel_id=1, source_target_pairs={{0,16},{8,24},{16,0},{24,8},{1,17},{9,25},{17,1},{25,9},{2,18},{10... | collective-permute-start | bytes 12296 | tf_op jit(solution)/shard_map/ppermute | solution.py:36
  257.0 6.3 %collective-permute-start.24 = (f32[2,512]{1,0:T(2,128)S(1)}, f32[2,512]{1,0:T(2,128)S(1)}, u32[]{:S(2)}, u32[]{:S(2)}) collective-permute-start(f32[2,512]{1,0:T(2,128)S(1)} %pad_maximum_fusion.1), channel_id=1, source_target_pairs={{0,8},{8,0},{16,24},{24,16},{1,9},{9,1},{17,25},{25,17},{2,10},{10... | collective-permute-start | bytes 12296 | tf_op jit(solution)/shard_map/ppermute | solution.py:36
  259.7 4.6 %collective-permute-start.43 = (f32[2,512]{1,0:T(2,128)S(1)}, f32[2,512]{1,0:T(2,128)S(1)}, u32[]{:S(2)}, u32[]{:S(2)}) collective-permute-start(f32[2,512]{1,0:T(2,128)S(1)} %pad_maximum_fusion.3), channel_id=1, source_target_pairs={{0,24},{8,16},{16,8},{24,0},{1,25},{9,17},{17,9},{25,1},{2,26},{10... | collective-permute-start | bytes 12296 | tf_op jit(solution)/shard_map/ppermute | solution.py:36
  261.0 3.6 %collective-permute-start.42 = (f32[2,512]{1,0:T(2,128)S(1)}, f32[2,512]{1,0:T(2,128)S(1)}, u32[]{:S(2)}, u32[]{:S(2)}) collective-permute-start(f32[2,512]{1,0:T(2,128)S(1)} %pad_maximum_fusion.3), channel_id=1, source_target_pairs={{0,16},{8,24},{16,0},{24,8},{1,17},{9,25},{17,1},{25,9},{2,18},{10... | collective-permute-start | bytes 12296 | tf_op jit(solution)/shard_map/ppermute | solution.py:36
  262.0 3.6 %collective-permute-start.41 = (f32[2,512]{1,0:T(2,128)S(1)}, f32[2,512]{1,0:T(2,128)S(1)}, u32[]{:S(2)}, u32[]{:S(2)}) collective-permute-start(f32[2,512]{1,0:T(2,128)S(1)} %pad_maximum_fusion.3), channel_id=1, source_target_pairs={{0,8},{8,0},{16,24},{24,16},{1,9},{9,1},{17,25},{25,17},{2,10},{10... | collective-permute-start | bytes 12296 | tf_op jit(solution)/shard_map/ppermute | solution.py:36
  273.1 13.2 %collective-permute-start.34 = (bf16[128,416]{1,0:T(8,128)(2,1)}, bf16[128,416]{1,0:T(8,128)(2,1)S(1)}, u32[]{:S(2)}, u32[]{:S(2)}) collective-permute-start(bf16[128,416]{1,0:T(8,128)(2,1)} %get-tuple-element.32), channel_id=1, source_target_pairs={{0,24},{8,16},{16,8},{24,0},{1,25},{9,17},{17,9},{25,1},{2,26},{10... | collective-permute-start | bytes 319496 | tf_op jit(solution)/shard_map/ppermute | solution.py:36
  275.2 11.8 %collective-permute-start.33 = (bf16[128,416]{1,0:T(8,128)(2,1)}, bf16[128,416]{1,0:T(8,128)(2,1)S(1)}, u32[]{:S(2)}, u32[]{:S(2)}) collective-permute-start(bf16[128,416]{1,0:T(8,128)(2,1)} %get-tuple-element.31), channel_id=1, source_target_pairs={{0,16},{8,24},{16,0},{24,8},{1,17},{9,25},{17,1},{25,9},{2,18},{10... | collective-permute-start | bytes 319496 | tf_op jit(solution)/shard_map/ppermute | solution.py:36
  276.8 14.7 %copy-start.10 = (f32[128,416]{1,0:T(8,128)S(1)}, f32[128,416]{1,0:T(8,128)}, u32[]{:S(2)}) copy-start(f32[128,416]{1,0:T(8,128)} %get-tuple-element.29) | copy-start | bytes 638980
  276.8 14.7 %copy-start.19 = (f32[416]{0:T(512)S(1)}, f32[416]{0:T(512)}, u32[]{:S(2)}) copy-start(f32[416]{0:T(512)} %param.39) | copy-start | bytes 4996
  276.8 10.2 %collective-permute-start.32 = (bf16[128,416]{1,0:T(8,128)(2,1)}, bf16[128,416]{1,0:T(8,128)(2,1)S(1)}, u32[]{:S(2)}, u32[]{:S(2)}) collective-permute-start(bf16[128,416]{1,0:T(8,128)(2,1)} %get-tuple-element.30), channel_id=1, source_target_pairs={{0,8},{8,0},{16,24},{24,16},{1,9},{9,1},{17,25},{25,17},{2,10},{10... | collective-permute-start | bytes 319496 | tf_op jit(solution)/shard_map/ppermute | solution.py:36
  283.4 6.2 %collective-permute-start.46 = (bf16[128,416]{1,0:T(8,128)(2,1)}, bf16[128,416]{1,0:T(8,128)(2,1)S(1)}, u32[]{:S(2)}, u32[]{:S(2)}) collective-permute-start(bf16[128,416]{1,0:T(8,128)(2,1)} %get-tuple-element.40), channel_id=1, source_target_pairs={{0,24},{8,16},{16,8},{24,0},{1,25},{9,17},{17,9},{25,1},{2,26},{10... | collective-permute-start | bytes 319496 | tf_op jit(solution)/shard_map/ppermute | solution.py:36
  284.8 6.2 %collective-permute-start.45 = (bf16[128,416]{1,0:T(8,128)(2,1)}, bf16[128,416]{1,0:T(8,128)(2,1)S(1)}, u32[]{:S(2)}, u32[]{:S(2)}) collective-permute-start(bf16[128,416]{1,0:T(8,128)(2,1)} %get-tuple-element.39), channel_id=1, source_target_pairs={{0,16},{8,24},{16,0},{24,8},{1,17},{9,25},{17,1},{25,9},{2,18},{10... | collective-permute-start | bytes 319496 | tf_op jit(solution)/shard_map/ppermute | solution.py:36
  286.3 5.2 %collective-permute-start.44 = (bf16[128,416]{1,0:T(8,128)(2,1)}, bf16[128,416]{1,0:T(8,128)(2,1)S(1)}, u32[]{:S(2)}, u32[]{:S(2)}) collective-permute-start(bf16[128,416]{1,0:T(8,128)(2,1)} %get-tuple-element.38), channel_id=1, source_target_pairs={{0,8},{8,0},{16,24},{24,16},{1,9},{9,1},{17,25},{25,17},{2,10},{10... | collective-permute-start | bytes 319496 | tf_op jit(solution)/shard_map/ppermute | solution.py:36
  (10 other events, 28.8 us)
Sparse Core Ops, SparseCore 0:
  18.3 46.9 all-gather.5
  66.8 56.6 all-gather.3
